TPU v7x, 32 devices: a whole 2x2x4 slice. The times are simulated.
32 devices in a mesh: dp: 4 (over y, x), tensor: 8 (over z, core).
Axes of the slice: x: 2, y: 2, z: 4, core: 2. Of those that a mesh axis runs over, the one named last changes fastest.
Arguments:
- query_states: bfloat16 [1536, 4096], P('dp', 'tensor'), may hold values from -64 to 64
- key_states: bfloat16 [1536, 4096], P('dp', 'tensor'), may hold values from -12 to 12
- value_states: bfloat16 [1536, 4096], P('dp', 'tensor'), may hold values from -6 to 6
- residual: bfloat16 [1536, 4096], P('dp', 'tensor'), may hold values from -6 to 6
- norm_gains: float32 [4, 4096], replicated, may hold values from 0.1 to 1.9
- lang_labels: int32 [32], replicated, may hold values from 0 to 3
- doc_lengths: int32 [32, 4], replicated, may hold values from 1 to 32, 48 in all within a row
- destinations: int32 [32], replicated, may hold values from 0 to 3, as said below
- gate_weight: bfloat16 [4096, 14336], P(None, 'tensor'), may hold values from -0.09375 to 0.09375
- up_weight: bfloat16 [4096, 14336], P(None, 'tensor'), may hold values from -0.09375 to 0.09375
- down_weight: bfloat16 [14336, 4096], P('tensor'), may hold values from -0.046875 to 0.046875
- out_cotangent: bfloat16 [1536, 4096], P(('dp', 'tensor')), may hold values from -6 to 6
Outputs:
- layer_out: bfloat16 [1536, 4096], P(('dp', 'tensor'))
- input_grad: bfloat16 [1536, 4096], P(('dp', 'tensor'))
- gate_grad: bfloat16 [4096, 14336], P('dp', 'tensor')
- up_grad: bfloat16 [4096, 14336], P('dp', 'tensor')
- down_grad: bfloat16 [14336, 4096], P('tensor', 'dp')
Inputs may be any that keep to these rules, and one draw needn't show every extreme that they name: `destinations`: every data group receives exactly 8 units. One group sends at most 2 units to any one group, and every group sends exactly 2 units to some group.
All inputs are finite; a program needn't handle non-finite values.
Results may differ from a plain program's by a relative error of at most 0.015.
Values may be sent and summed in bfloat16 or wider, within the bound.
A program may use at most 192 MiB of HBM per device.

v0:
```python
import math

import jax
import jax.numpy as jnp
from jax import lax
from jax.sharding import PartitionSpec as P

HD = 128
UNIT = 48
CAP = 2
WIN = 24


def doc_index(doc_lengths, unit_len):
    doc_ends = jnp.cumsum(doc_lengths, axis=1)
    positions = jnp.arange(unit_len, dtype=jnp.int32)
    return jnp.sum((doc_ends[:, None, :] <= positions[None, :, None]).astype(jnp.int32), axis=2)


def attend(query_units, key_units, value_units, resid_units, doc_units):
    unit_count, unit_len, columns = query_units.shape
    head_shape = (unit_count, unit_len, columns // HD, HD)
    scores = jnp.einsum(
        "uqhd,ukhd->uhqk",
        query_units.reshape(head_shape),
        key_units.reshape(head_shape),
        preferred_element_type=jnp.float32,
    ) / math.sqrt(HD)
    positions = jnp.arange(unit_len, dtype=jnp.int32)
    distance = positions[:, None] - positions[None, :]
    allowed = (doc_units[:, :, None] == doc_units[:, None, :]) & (
        (distance >= 0) & (distance < WIN)
    )[None]
    scores = jnp.where(allowed[:, None], scores, -1e30)
    row_max = jnp.max(scores, axis=3, keepdims=True)
    exp_scores = jnp.exp(scores - row_max)
    attn_probs = (exp_scores / jnp.sum(exp_scores, axis=3, keepdims=True)).astype(jnp.bfloat16)
    mixed_heads = jnp.einsum(
        "uhqk,ukhd->uqhd",
        attn_probs,
        value_units.reshape(head_shape),
        preferred_element_type=jnp.float32,
    )
    return (
        resid_units.astype(jnp.float32) + mixed_heads.reshape(unit_count, unit_len, columns)
    ).astype(jnp.bfloat16)


def pack_units(send_table, unit_data):
    return jnp.einsum(
        "tsu,uic->tsic", send_table, unit_data, preferred_element_type=jnp.float32
    ).astype(jnp.bfloat16)


def unpack_units(recv_table, arrived):
    return jnp.einsum(
        "jts,tsic->jic", recv_table, arrived, preferred_element_type=jnp.float32
    ).astype(jnp.bfloat16)


def per_device(
    query_states,
    key_states,
    value_states,
    residual,
    norm_gains,
    lang_labels,
    doc_lengths,
    destinations,
    gate_weight,
    up_weight,
    down_weight,
    out_cotangent,
):
    groups = lax.axis_size("dp")
    my_group = lax.axis_index("dp")
    total_units = destinations.shape[0]
    per_group = total_units // groups
    columns = query_states.shape[1]
    width_d = gate_weight.shape[0]
    hidden_here = gate_weight.shape[1]
    tok_group = per_group * UNIT
    doc_ids = doc_index(doc_lengths, UNIT)
    unit_index = jnp.arange(total_units, dtype=jnp.int32)
    source_group = unit_index // per_group
    earlier = unit_index[None, :] < unit_index[:, None]
    same_target = destinations[None, :] == destinations[:, None]
    same_source = source_group[None, :] == source_group[:, None]
    send_rank = jnp.sum((earlier & same_target & same_source).astype(jnp.int32), axis=1)
    arrival = jnp.sum((earlier & same_target).astype(jnp.int32), axis=1)
    first_unit = my_group * per_group
    own_targets = lax.dynamic_slice_in_dim(destinations, first_unit, per_group)
    own_ranks = lax.dynamic_slice_in_dim(send_rank, first_unit, per_group)
    group_ids = jnp.arange(groups, dtype=jnp.int32)
    slot_ids = jnp.arange(CAP, dtype=jnp.int32)
    send_table = (
        (own_targets[None, None, :] == group_ids[:, None, None])
        & (own_ranks[None, None, :] == slot_ids[None, :, None])
    ).astype(jnp.bfloat16)
    arrive_ids = jnp.arange(per_group, dtype=jnp.int32)
    landing = (destinations == my_group)[None, :] & (arrival[None, :] == arrive_ids[:, None])
    recv_table = jnp.sum(
        (
            landing[:, None, None, :]
            & (source_group[None, None, None, :] == group_ids[None, :, None, None])
            & (send_rank[None, None, None, :] == slot_ids[None, None, :, None])
        ).astype(jnp.int32),
        axis=3,
    ).astype(jnp.bfloat16)
    landing_int = landing.astype(jnp.int32)
    moved_langs = jnp.sum(landing_int * lang_labels[None, :], axis=1)
    unit_shape = (per_group, UNIT, columns)
    moved_docs = jnp.sum(landing_int[:, :, None] * doc_ids[None, :, :], axis=1)
    moved_pack = (
        lax.all_to_all(
            pack_units(send_table, query_states.reshape(unit_shape)),
            "dp",
            split_axis=0,
            concat_axis=0,
            tiled=True,
        ),
        lax.all_to_all(
            pack_units(send_table, key_states.reshape(unit_shape)),
            "dp",
            split_axis=0,
            concat_axis=0,
            tiled=True,
        ),
        lax.all_to_all(
            pack_units(send_table, value_states.reshape(unit_shape)),
            "dp",
            split_axis=0,
            concat_axis=0,
            tiled=True,
        ),
        lax.all_to_all(
            pack_units(send_table, residual.reshape(unit_shape)),
            "dp",
            split_axis=0,
            concat_axis=0,
            tiled=True,
        ),
    )
    mixed_units = attend(
        unpack_units(recv_table, moved_pack[0]),
        unpack_units(recv_table, moved_pack[1]),
        unpack_units(recv_table, moved_pack[2]),
        unpack_units(recv_table, moved_pack[3]),
        moved_docs,
    )
    stream_cols = mixed_units.reshape(tok_group, columns)
    lang_tokens = jnp.broadcast_to(moved_langs[:, None], (per_group, UNIT)).reshape(tok_group)
    lang_onehot = (
        lang_tokens[:, None] == jnp.arange(norm_gains.shape[0], dtype=jnp.int32)[None, :]
    ).astype(jnp.float32)
    col_block = lax.all_gather(stream_cols, "tensor", axis=1, tiled=True)
    gain_block = jnp.dot(lang_onehot, norm_gains, precision=lax.Precision.HIGHEST)
    block_f = col_block.astype(jnp.float32)
    scaled_block = (block_f * gain_block).astype(jnp.bfloat16)
    gate_rows = gate_weight
    up_rows = up_weight
    gate_acc = jnp.dot(scaled_block, gate_rows, preferred_element_type=jnp.float32)
    up_acc = jnp.dot(scaled_block, up_rows, preferred_element_type=jnp.float32)
    stream_full = col_block
    squares = jnp.sum(block_f * block_f, axis=1)
    gate_acc, up_acc, stream_full, squares = (gate_acc, up_acc, stream_full, squares)
    inv_rms = lax.rsqrt(squares / width_d + 1e-05)
    act_gate = inv_rms[:, None] * gate_acc
    act_up = inv_rms[:, None] * up_acc
    hidden = (jax.nn.silu(act_gate) * act_up).astype(jnp.bfloat16)
    gain_tokens = jnp.dot(lang_onehot, norm_gains, precision=lax.Precision.HIGHEST)
    scaled_full = (stream_full.astype(jnp.float32) * gain_tokens).astype(jnp.bfloat16)
    row_block = lax.all_gather(out_cotangent, "tensor", axis=0, tiled=True)
    row_part = lax.dot_general(
        row_block, down_weight, (((1,), (1,)), ((), ())), preferred_element_type=jnp.float32
    )
    sigma = jax.nn.sigmoid(act_gate)
    grad_gate = (
        inv_rms[:, None] * row_part * act_up * sigma * (1.0 + act_gate * (1.0 - sigma))
    ).astype(jnp.bfloat16)
    grad_up = (inv_rms[:, None] * row_part * jax.nn.silu(act_gate)).astype(jnp.bfloat16)
    rows_here = out_cotangent.shape[0]
    gate_rows = grad_gate
    up_rows = grad_up
    out_part = jnp.dot(hidden, down_weight, preferred_element_type=jnp.float32)
    back_part = lax.dot_general(
        gate_rows, gate_weight, (((1,), (1,)), ((), ())), preferred_element_type=jnp.float32
    ) + lax.dot_general(
        up_rows, up_weight, (((1,), (1,)), ((), ())), preferred_element_type=jnp.float32
    )
    row_totals = lax.psum_scatter(
        jnp.concatenate([out_part, back_part], axis=1).astype(jnp.bfloat16),
        "tensor",
        scatter_dimension=0,
        tiled=True,
    ).astype(jnp.float32)
    my_start = lax.axis_index("tensor") * rows_here
    stream_rows = lax.dynamic_slice_in_dim(stream_full, my_start, rows_here, 0).astype(jnp.float32)
    scaled_rows = lax.dynamic_slice_in_dim(scaled_full, my_start, rows_here, 0).astype(jnp.float32)
    gain_rows = lax.dynamic_slice_in_dim(gain_tokens, my_start, rows_here, 0)
    rms_rows = lax.dynamic_slice_in_dim(inv_rms, my_start, rows_here, 0)
    out_total = row_totals[:, :width_d]
    back_total = row_totals[:, width_d:]
    layer_out = (stream_rows + out_total).astype(jnp.bfloat16)
    dot_sum = jnp.sum(scaled_rows * back_total, axis=1)
    input_grad = (
        out_cotangent.astype(jnp.float32)
        + gain_rows * back_total
        - (rms_rows * rms_rows / width_d)[:, None] * stream_rows * dot_sum[:, None]
    ).astype(jnp.bfloat16)
    factors = jnp.concatenate([grad_gate, grad_up], axis=1)
    share_rows = width_d // groups
    scaled_split = scaled_full.reshape(tok_group, groups, share_rows)
    cot_split = row_block.reshape(tok_group, groups, share_rows)
    token_side = jnp.concatenate([factors, hidden], axis=1)
    token_copies = jnp.broadcast_to(token_side[:, None, :], (tok_group, groups, 3 * hidden_here))
    scaled_recv, cot_recv, token_recv = (
        lax.all_to_all(scaled_split, "dp", split_axis=1, concat_axis=1, tiled=True),
        lax.all_to_all(cot_split, "dp", split_axis=1, concat_axis=1, tiled=True),
        lax.all_to_all(token_copies, "dp", split_axis=1, concat_axis=1, tiled=True),
    )
    gate_up_parts = jnp.einsum(
        "tgd,tgf->gdf",
        scaled_recv,
        token_recv[:, :, : 2 * hidden_here],
        preferred_element_type=jnp.float32,
    ).astype(jnp.bfloat16)
    down_parts = jnp.einsum(
        "tgd,tgf->gdf",
        cot_recv,
        token_recv[:, :, 2 * hidden_here :],
        preferred_element_type=jnp.float32,
    ).astype(jnp.bfloat16)
    gate_up_parts, down_parts = lax.optimization_barrier((gate_up_parts, down_parts))
    summed = jnp.concatenate(
        [
            jnp.sum(gate_up_parts.astype(jnp.float32), axis=0),
            jnp.sum(down_parts.astype(jnp.float32), axis=0),
        ],
        axis=1,
    )
    gate_grad = summed[:, :hidden_here].astype(jnp.bfloat16)
    up_grad = summed[:, hidden_here : 2 * hidden_here].astype(jnp.bfloat16)
    down_grad = summed[:, 2 * hidden_here :].T.astype(jnp.bfloat16)
    return (layer_out, input_grad, gate_grad, up_grad, down_grad)


def solution(mesh):
    return jax.shard_map(
        per_device,
        mesh=mesh,
        in_specs=(
            P("dp", "tensor"),
            P("dp", "tensor"),
            P("dp", "tensor"),
            P("dp", "tensor"),
            P(),
            P(),
            P(),
            P(),
            P(None, "tensor"),
            P(None, "tensor"),
            P("tensor", None),
            P(("dp", "tensor"), None),
        ),
        out_specs=(
            P(("dp", "tensor"), None),
            P(("dp", "tensor"), None),
            P("dp", "tensor"),
            P("dp", "tensor"),
            P("tensor", "dp"),
        ),
        check_vma=False,
    )
```

profile of v0, /device:TPU:0, one launch (start us, length us, event | category | flops | bytes accessed | tf_op | source)
XLA Modules:
  0.0 451.7 jit_solution(4844649436093830645)
XLA Ops:
  11.1 5.2 %all-to-all-start.1 = ((bf16[4,2,48,512]{3,1,2,0:T(2,128)(2,1)}), bf16[4,2,48,512]{3,1,2,0:T(2,128)(2,1)S(1)}, u32[]{:S(2)}, u32[]{:S(2)}) async-start(bf16[4,2,48,512]{3,1,2,0:T(2,128)(2,1)} %copy.64), calls=%async_computation.1 | async-start | bytes 786432 | tf_op jit(solution)/shard_map/all_to_all | solution.py:129
  23.4 4.2 all-to-all-start.2
  27.7 5.9 %all-to-all-done.2 = bf16[4,2,48,512]{3,1,2,0:T(2,128)(2,1)S(1)} async-done(((bf16[4,2,48,512]{3,1,2,0:T(2,128)(2,1)}), bf16[4,2,48,512]{3,1,2,0:T(2,128)(2,1)S(1)}, u32[]{:S(2)}, u32[]{:S(2)}) %all-to-all-start.2) | async-done | bytes 393248 | tf_op jit(solution)/shard_map/all_to_all | solution.py:115
  38.3 4.6 %all-to-all-done.3 = bf16[4,2,48,512]{3,1,2,0:T(2,128)(2,1)S(1)} async-done(((bf16[4,2,48,512]{3,1,2,0:T(2,128)(2,1)}), bf16[4,2,48,512]{3,1,2,0:T(2,128)(2,1)S(1)}, u32[]{:S(2)}, u32[]{:S(2)}) %all-to-all-start.3) | async-done | bytes 393248 | tf_op jit(solution)/shard_map/all_to_all | solution.py:122
  48.2 4.0 all-to-all-done
  60.6 5.0 %all-to-all-start.6 = ((bf16[384,4,1024]{2,0,1:T(8,128)(2,1)}), bf16[384,4,1024]{2,0,1:T(8,128)(2,1)}, u32[]{:S(2)}, u32[]{:S(2)}) async-start(bf16[384,4,1024]{2,0,1:T(8,128)(2,1)} %copy.83), calls=%async_computation.7 | async-start | bytes 6291456 | tf_op jit(solution)/shard_map/all_to_all | solution.py:219
  65.6 27.2 %all-gather.3.cloned.1.call-done = bf16[384,4096]{1,0:T(8,128)(2,1)} async-done(((bf16[384,512]{1,0:T(8,128)(2,1)}), bf16[384,4096]{1,0:T(8,128)(2,1)}) %all-gather.3.cloned.1.call-update) | async-done | bytes 3145744 | tf_op jit(solution)/shard_map/all_gather | solution.py:156
  92.8 6.6 %fusion.2 = (f32[384]{0:T(512)S(1)}, bf16[384,4096]{1,0:T(8,128)(2,1)S(1)}, f32[384,4096]{1,0:T(8,128)}) fusion(bf16[384,4096]{1,0:T(8,128)(2,1)} %all-gather.3.cloned.1.call-done, f32[4,4096]{1,0:T(4,128)S(1)} %copy-done.10, s32[384]{0:T(512)S(1)} %eq.183), kind=kOutput, calls=%fused_computation.6 | convolution fusion | flops 83362944 | bytes 12651520 | tf_op jit(solution)/shard_map/dot_general | solution.py:157
  99.4 11.0 %convolution_multiply_fusion.2 = f32[384,1792]{1,0:T(8,128)} fusion(bf16[384,4096]{1,0:T(8,128)(2,1)S(1)} %get-tuple-element.19, bf16[4096,1792]{1,0:T(8,128)(2,1)} %param.20, f32[384]{0:T(512)S(1)} %add_rsqrt_fusion), kind=kOutput, calls=%fused_computation.15 | convolution fusion | flops 5637832704 | bytes 20579840 | tf_op jit(solution)/shard_map/dot_general | solution.py:162
  110.4 11.0 %convolution_multiply_fusion = f32[384,1792]{1,0:T(8,128)} fusion(bf16[384,4096]{1,0:T(8,128)(2,1)S(1)} %copy-done.2, bf16[1792,4096]{1,0:T(8,128)(2,1)} %param.22, f32[384]{0:T(512)S(1)} %add_rsqrt_fusion), kind=kOutput, calls=%fused_computation.13 | convolution fusion | flops 5637832704 | bytes 20579840 | tf_op jit(solution)/shard_map/dot_general | solution.py:174
  121.4 12.6 %multiply_convert_fusion.2 = (bf16[384,1792]{1,0:T(8,128)(2,1)S(1)}, bf16[384,1792]{1,0:T(8,128)(2,1)S(1)}, bf16[384,1792]{1,0:T(8,128)(2,1)S(1)}) fusion(f32[384,1792]{1,0:T(8,128)} %convolution_multiply_fusion.2, f32[384,1792]{1,0:T(8,128)} %convolution_multiply_fusion, bf16[384,4096]{1,0:T(8,128)(2,1)S(1)} %get-tuple-element.19, ...), kind=kOutput, calls=%fused_computation.18 | convolution fusion | flops 5648154624 | bytes 27461120 | tf_op jit(solution)/shard_map/dot_general | solution.py:163
  136.9 12.8 %convolution_convert_fusion.1 = bf16[384,4096]{1,0:T(8,128)(2,1)} fusion(bf16[384,1792]{1,0:T(8,128)(2,1)S(1)} %get-tuple-element.13, bf16[1792,4096]{1,0:T(8,128)(2,1)} %param.22), kind=kOutput, calls=%fused_computation.10 | convolution fusion | flops 5638717440 | bytes 19202048 | tf_op jit(solution)/shard_map/dot_general | solution.py:185
  149.7 7.3 %broadcast_in_dim.15 = bf16[384,4,5376]{2,0,1:T(8,128)(2,1)} broadcast(bf16[384,5376]{1,0:T(8,128)(2,1)} %pad_maximum_fusion.1), dimensions={0,2} | broadcast | bytes 20643840 | tf_op jit(solution)/shard_map/broadcast_in_dim | solution.py:216
  157.0 6.9 %all-to-all-start.5 = ((bf16[384,4,5376]{2,0,1:T(8,128)(2,1)}), bf16[384,4,5376]{2,0,1:T(8,128)(2,1)}, u32[]{:S(2)}, u32[]{:S(2)}) async-start(bf16[384,4,5376]{2,0,1:T(8,128)(2,1)} %broadcast_in_dim.15), calls=%async_computation.6 | async-start | bytes 33030144 | tf_op jit(solution)/shard_map/all_to_all | solution.py:220
  164.0 11.3 %fusion.62 = f32[384,4096]{1,0:T(8,128)} fusion(bf16[384,1792]{1,0:T(8,128)(2,1)} %copy-done.7, bf16[4096,1792]{1,0:T(8,128)(2,1)} %param.20), kind=kOutput, calls=%fused_computation.115 | convolution fusion | flops 5637144576 | bytes 22347776 | tf_op jit(solution)/shard_map/dot_general | solution.py:186
  175.3 20.5 %add_convert_fusion = bf16[384,4096]{1,0:T(8,128)(2,1)S(1)} fusion(f32[384,4096]{1,0:T(8,128)} %fusion.62, bf16[384,1792]{1,0:T(8,128)(2,1)S(1)} %copy-done.6, bf16[4096,1792]{1,0:T(8,128)(2,1)} %param.21), kind=kOutput, calls=%fused_computation.9 | convolution fusion | flops 5640290304 | bytes 25493504 | tf_op jit(solution)/shard_map/dot_general | solution.py:188
  202.0 142.0 %all-to-all-done.5 = bf16[384,4,5376]{2,0,1:T(8,128)(2,1)} async-done(((bf16[384,4,5376]{2,0,1:T(8,128)(2,1)}), bf16[384,4,5376]{2,0,1:T(8,128)(2,1)}, u32[]{:S(2)}, u32[]{:S(2)}) %all-to-all-start.5) | async-done | bytes 16515104 | tf_op jit(solution)/shard_map/all_to_all | solution.py:220
  344.0 4.9 %all-to-all-start.4 = ((bf16[384,4,1024]{0,2,1:T(8,128)(2,1)}), bf16[384,4,1024]{0,2,1:T(8,128)(2,1)}, u32[]{:S(2)}, u32[]{:S(2)}) async-start(bf16[384,4,1024]{0,2,1:T(8,128)(2,1)} %bitcast.116), calls=%async_computation.5 | async-start | bytes 6291456 | tf_op jit(solution)/shard_map/all_to_all | solution.py:218
  349.0 13.7 %convert_bitcast_fusion = bf16[4,1024,1792]{1,2,0:T(8,128)(2,1)} fusion(bf16[384,4,1024]{2,0,1:T(8,128)(2,1)} %all-to-all-done.6, bf16[384,4,5376]{2,0,1:T(8,128)(2,1)} %all-to-all-done.5), kind=kOutput, calls=%fused_computation.2 | convolution fusion | flops 5644484608 | bytes 23330816 | tf_op jit(solution)/shard_map/tgd,tgf->gdf/dot_general | solution.py:228
  362.7 22.2 %all-to-all-done.4 = bf16[384,4,1024]{0,2,1:T(8,128)(2,1)} async-done(((bf16[384,4,1024]{0,2,1:T(8,128)(2,1)}), bf16[384,4,1024]{0,2,1:T(8,128)(2,1)}, u32[]{:S(2)}, u32[]{:S(2)}) %all-to-all-start.4) | async-done | bytes 3145760 | tf_op jit(solution)/shard_map/all_to_all | solution.py:218
  384.9 23.3 %convolution_convert_fusion = bf16[4,1024,3584]{2,1,0:T(8,128)(2,1)} fusion(bf16[384,4,1024]{0,2,1:T(8,128)(2,1)} %all-to-all-done.4, bf16[384,4,5376]{2,0,1:T(8,128)(2,1)} %all-to-all-done.5), kind=kOutput, calls=%fused_computation.1 | convolution fusion | flops 11288969216 | bytes 43515904 | tf_op jit(solution)/shard_map/tgd,tgf->gdf/dot_general | solution.py:222
  408.2 14.9 %reduce.1 = bf16[1024,3584]{1,0:T(8,128)(2,1)} reduce(bf16[4,1024,3584]{2,1,0:T(8,128)(2,1)} %convolution_convert_fusion, bf16[]{:T(256)} %constant.67.clone.1), dimensions={0}, to_apply=%region_12.13.clone | reduce | flops 11010048 | bytes 36700160 | tf_op jit(solution)/shard_map/reduce_sum | solution.py:237
  423.2 11.0 %reduce_sum.112 = bf16[1024,1792]{0,1:T(8,128)(2,1)} reduce(bf16[4,1024,1792]{1,2,0:T(8,128)(2,1)} %convert_bitcast_fusion, bf16[]{:T(256)} %constant.67.clone.1), dimensions={0}, to_apply=%region_13.14 | reduce | flops 5505024 | bytes 18350082 | tf_op jit(solution)/shard_map/reduce_sum | solution.py:238
  434.1 6.7 %fusion.60 = (bf16[1024,1792]{1,0:T(8,128)(2,1)}, bf16[1024,1792]{1,0:T(8,128)(2,1)}) fusion(bf16[1024,3584]{1,0:T(8,128)(2,1)} %reduce.1), kind=kLoop, calls=%fused_computation.113 | loop fusion | bytes 14680064 | tf_op jit(solution)/shard_map/slice | solution.py:243
  (83 shorter events, 42.6 us)
Async XLA Ops:
  7.2 2.5 copy-start
  7.2 11.8 %copy-start.8 = (bf16[384,512]{1,0:T(8,128)(2,1)S(1)}, bf16[384,512]{1,0:T(8,128)(2,1)}, u32[]{:S(2)}) copy-start(bf16[384,512]{1,0:T(8,128)(2,1)} %param.13) | copy-start | bytes 1179652
  7.2 12.2 %copy-start.9 = (bf16[384,512]{1,0:T(8,128)(2,1)S(1)}, bf16[384,512]{1,0:T(8,128)(2,1)}, u32[]{:S(2)}) copy-start(bf16[384,512]{1,0:T(8,128)(2,1)} %param.15) | copy-start | bytes 1179652
  7.2 47.1 %all-gather.5.cloned.1.call-start = ((), (), s32[]{:S(2)}) async-start(), calls=%async_computation.9 | async-start | bytes 3538944 | tf_op jit(solution)/shard_map/all_gather | solution.py:173
  11.1 12.2 %all-to-all-start.1 = ((bf16[4,2,48,512]{3,1,2,0:T(2,128)(2,1)}), bf16[4,2,48,512]{3,1,2,0:T(2,128)(2,1)S(1)}, u32[]{:S(2)}, u32[]{:S(2)}) async-start(bf16[4,2,48,512]{3,1,2,0:T(2,128)(2,1)} %copy.64), calls=%async_computation.1 | async-start | bytes 786432 | tf_op jit(solution)/shard_map/all_to_all | solution.py:129
  23.4 10.2 %all-to-all-start.2 = ((bf16[4,2,48,512]{3,1,2,0:T(2,128)(2,1)}), bf16[4,2,48,512]{3,1,2,0:T(2,128)(2,1)S(1)}, u32[]{:S(2)}, u32[]{:S(2)}) async-start(bf16[4,2,48,512]{3,1,2,0:T(2,128)(2,1)} %copy.68), calls=%async_computation.2 | async-start | bytes 786432 | tf_op jit(solution)/shard_map/all_to_all | solution.py:115
  33.6 9.3 %all-to-all-start.3 = ((bf16[4,2,48,512]{3,1,2,0:T(2,128)(2,1)}), bf16[4,2,48,512]{3,1,2,0:T(2,128)(2,1)S(1)}, u32[]{:S(2)}, u32[]{:S(2)}) async-start(bf16[4,2,48,512]{3,1,2,0:T(2,128)(2,1)} %copy.72), calls=%async_computation.3 | async-start | bytes 786432 | tf_op jit(solution)/shard_map/all_to_all | solution.py:122
  42.9 9.3 %all-to-all-start = ((bf16[4,2,48,512]{3,1,2,0:T(2,128)(2,1)}), bf16[4,2,48,512]{3,1,2,0:T(2,128)(2,1)S(1)}, u32[]{:S(2)}, u32[]{:S(2)}) async-start(bf16[4,2,48,512]{3,1,2,0:T(2,128)(2,1)} %copy.60), calls=%async_computation | async-start | bytes 786432 | tf_op jit(solution)/shard_map/all_to_all | solution.py:136
  46.3 46.4 %all-gather.3.cloned.1.call-start = ((), (), s32[]{:S(2)}) async-start(), calls=%async_computation.8 | async-start | bytes 3538944 | tf_op jit(solution)/shard_map/all_gather | solution.py:156
  47.8 6.3 %copy-start.11 = (s32[32]{0:T(128)S(1)}, s32[32]{0:T(128)}, u32[]{:S(2)}) copy-start(s32[32]{0:T(128)} %param.17) | copy-start | bytes 388
  60.6 32.2 %copy-start.10 = (f32[4,4096]{1,0:T(4,128)S(1)}, f32[4,4096]{1,0:T(4,128)}, u32[]{:S(2)}) copy-start(f32[4,4096]{1,0:T(4,128)} %param.16) | copy-start | bytes 196612
  60.6 89.1 %all-to-all-start.6 = ((bf16[384,4,1024]{2,0,1:T(8,128)(2,1)}), bf16[384,4,1024]{2,0,1:T(8,128)(2,1)}, u32[]{:S(2)}, u32[]{:S(2)}) async-start(bf16[384,4,1024]{2,0,1:T(8,128)(2,1)} %copy.83), calls=%async_computation.7 | async-start | bytes 6291456 | tf_op jit(solution)/shard_map/all_to_all | solution.py:219
  99.4 11.0 %copy-start.2 = (bf16[384,4096]{1,0:T(8,128)(2,1)S(1)}, bf16[384,4096]{1,0:T(8,128)(2,1)}, u32[]{:S(2)}) copy-start(bf16[384,4096]{1,0:T(8,128)(2,1)} %all-gather.5.cloned.1.call-done) | copy-start | bytes 9437188
  134.0 2.3 copy-start.5
  134.0 2.8 copy-start.7
  157.0 187.0 %all-to-all-start.5 = ((bf16[384,4,5376]{2,0,1:T(8,128)(2,1)}), bf16[384,4,5376]{2,0,1:T(8,128)(2,1)}, u32[]{:S(2)}, u32[]{:S(2)}) async-start(bf16[384,4,5376]{2,0,1:T(8,128)(2,1)} %broadcast_in_dim.15), calls=%async_computation.6 | async-start | bytes 33030144 | tf_op jit(solution)/shard_map/all_to_all | solution.py:220
  163.9 276.9 %reduce-scatter.2.cloned.1.call-start = ((), (), s32[]{:S(2)}) async-start(), calls=%async_computation.10 | async-start | bytes 7077888 | tf_op jit(solution)/shard_map/reduce_scatter | solution.py:191
  164.0 11.4 %copy-start.6 = (bf16[384,1792]{1,0:T(8,128)(2,1)S(1)}, bf16[384,1792]{1,0:T(8,128)(2,1)}, u32[]{:S(2)}) copy-start(bf16[384,1792]{1,0:T(8,128)(2,1)} %copy-done.5) | copy-start | bytes 4128772
  175.3 20.5 %copy-start.3 = (bf16[384,4096]{1,0:T(8,128)(2,1)S(1)}, bf16[384,4096]{1,0:T(8,128)(2,1)}, u32[]{:S(2)}) copy-start(bf16[384,4096]{1,0:T(8,128)(2,1)} %convolution_convert_fusion.1) | copy-start | bytes 9437188
  344.0 40.9 %all-to-all-start.4 = ((bf16[384,4,1024]{0,2,1:T(8,128)(2,1)}), bf16[384,4,1024]{0,2,1:T(8,128)(2,1)}, u32[]{:S(2)}, u32[]{:S(2)}) async-start(bf16[384,4,1024]{0,2,1:T(8,128)(2,1)} %bitcast.116), calls=%async_computation.5 | async-start | bytes 6291456 | tf_op jit(solution)/shard_map/all_to_all | solution.py:218
  440.8 1.5 copy-start.4
  440.8 4.0 copy-start.1
Sparse Core Ops, SparseCore 0:
  9.7 40.9 all-gather.4
  54.1 38.5 all-gather.2
  199.3 69.1 reduce-scatter.1
where the time goes:
time: 459 us; the launch traced here: 452 us
  waiting for transfers between devices  206 us (45%)
  matrix products  129 us (28%)
  other arithmetic  38.8 us (8%)
  starting transfers between devices  33.2 us (7%)
  local copies, waits for them, and re-layouts  29.7 us (6%)
  between operations  14.5 us (3%)
    all_to_all x1, waiting for transfers between devices, per_device(): lax.all_to_all(token_copies, 'dp', split_axis=1, concat_axis=1, tiled=True)  142 us
    all_gather x1, waiting for transfers between devices, per_device(): col_block = lax.all_gather(stream_cols, 'tensor', axis=1, tiled=True)  27.2 us
    dot_general x1, matrix products, per_device(): jnp.einsum('tgd,tgf->gdf', scaled_recv, token_recv[:, :, :2 * hidden_here...  23.3 us
    all_to_all x1, waiting for transfers between devices, per_device(): lax.all_to_all(scaled_split, 'dp', split_axis=1, concat_axis=1, tiled=True)  22.2 us
    dot_general x1, matrix products, per_device(): lax.dot_general(up_rows, up_weight, (((1,), (1,)), ((), ())), preferred_e...  20.5 us
    reduce_sum x1, other arithmetic, per_device(): jnp.sum(gate_up_parts.astype(jnp.float32), axis=0)  14.9 us
    dot_general x1, matrix products, per_device(): jnp.einsum('tgd,tgf->gdf', cot_recv, token_recv[:, :, 2 * hidden_here:],...  13.7 us
    dot_general x1, matrix products, per_device(): out_part = jnp.dot(hidden, down_weight, preferred_element_type=jnp.float32)  12.8 us
  transfers between devices with their start and end apart: 10, of which 6 were waited for; matrix products, arithmetic and copies ran while one was open for 41% of the time, Pallas kernels for 0%

commit v1 on v0

v1 whole, which is shorter than its diff:
```python
import math

import jax
import jax.numpy as jnp
from jax import lax
from jax.sharding import PartitionSpec as P

HD = 128
UNIT = 48
CAP = 2
WIN = 24


def doc_index(doc_lengths, unit_len):
    doc_ends = jnp.cumsum(doc_lengths, axis=1)
    positions = jnp.arange(unit_len, dtype=jnp.int32)
    return jnp.sum((doc_ends[:, None, :] <= positions[None, :, None]).astype(jnp.int32), axis=2)


def attend(query_units, key_units, value_units, resid_units, doc_units):
    unit_count, unit_len, columns = query_units.shape
    head_shape = (unit_count, unit_len, columns // HD, HD)
    scores = jnp.einsum(
        "uqhd,ukhd->uhqk",
        query_units.reshape(head_shape),
        key_units.reshape(head_shape),
        preferred_element_type=jnp.float32,
    ) / math.sqrt(HD)
    positions = jnp.arange(unit_len, dtype=jnp.int32)
    distance = positions[:, None] - positions[None, :]
    allowed = (doc_units[:, :, None] == doc_units[:, None, :]) & (
        (distance >= 0) & (distance < WIN)
    )[None]
    scores = jnp.where(allowed[:, None], scores, -1e30)
    row_max = jnp.max(scores, axis=3, keepdims=True)
    exp_scores = jnp.exp(scores - row_max)
    attn_probs = (exp_scores / jnp.sum(exp_scores, axis=3, keepdims=True)).astype(jnp.bfloat16)
    mixed_heads = jnp.einsum(
        "uhqk,ukhd->uqhd",
        attn_probs,
        value_units.reshape(head_shape),
        preferred_element_type=jnp.float32,
    )
    return (
        resid_units.astype(jnp.float32) + mixed_heads.reshape(unit_count, unit_len, columns)
    ).astype(jnp.bfloat16)


def pack_units(send_table, unit_data):
    return jnp.einsum(
        "tsu,uic->tsic", send_table, unit_data, preferred_element_type=jnp.float32
    ).astype(jnp.bfloat16)


def unpack_units(recv_table, arrived):
    return jnp.einsum(
        "jts,tsic->jic", recv_table, arrived, preferred_element_type=jnp.float32
    ).astype(jnp.bfloat16)


def exchange(block, distance):
    groups = lax.axis_size("dp")
    return lax.ppermute(block, "dp", [(i, i ^ distance) for i in range(groups)])


def first_hops(block):
    groups = lax.axis_size("dp")
    distances = (1, 2) if groups == 4 else range(1, groups)
    return [exchange(block, o) for o in distances]


def second_hops(arrived):
    if lax.axis_size("dp") != 4:
        return []
    half = arrived[0].shape[0] // 2
    return [exchange(arrived[0][:half], 2), exchange(arrived[1][half:], 1)]


def after(value, *earlier):
    return lax.optimization_barrier((value, *earlier))


def deal(block, share):
    groups = lax.axis_size("dp")
    me = lax.axis_index("dp")
    parts = []
    for o in range(groups):
        piece = lax.dynamic_slice_in_dim(block, (me ^ o) * share, share, 1)
        parts.append(piece if o == 0 else exchange(piece, o))
    return parts


def pick_gains(langs, norm_gains):
    gains = jnp.zeros((langs.shape[0], norm_gains.shape[1]), jnp.float32)
    for index in range(norm_gains.shape[0]):
        gains = jnp.where((langs == index)[:, None], norm_gains[index][None, :], gains)
    return gains


def per_device(
    query_states,
    key_states,
    value_states,
    residual,
    norm_gains,
    lang_labels,
    doc_lengths,
    destinations,
    gate_weight,
    up_weight,
    down_weight,
    out_cotangent,
):
    groups = lax.axis_size("dp")
    shards = lax.axis_size("tensor")
    my_group = lax.axis_index("dp")
    total_units = destinations.shape[0]
    per_group = total_units // groups
    columns = query_states.shape[1]
    width_d = gate_weight.shape[0]
    share = width_d // groups
    tok_group = per_group * UNIT
    rows_here = out_cotangent.shape[0]
    first_unit = my_group * per_group

    cot_full = lax.all_gather(out_cotangent, "tensor", axis=0, tiled=True)

    own_docs = doc_index(lax.dynamic_slice_in_dim(doc_lengths, first_unit, per_group), UNIT)
    unit_shape = (per_group, UNIT, columns)
    mixed_units = attend(
        query_states.reshape(unit_shape),
        key_states.reshape(unit_shape),
        value_states.reshape(unit_shape),
        residual.reshape(unit_shape),
        own_docs,
    )

    unit_index = jnp.arange(total_units, dtype=jnp.int32)
    source_group = unit_index // per_group
    earlier = unit_index[None, :] < unit_index[:, None]
    same_target = destinations[None, :] == destinations[:, None]
    same_source = source_group[None, :] == source_group[:, None]
    send_rank = jnp.sum((earlier & same_target & same_source).astype(jnp.int32), axis=1)
    arrival = jnp.sum((earlier & same_target).astype(jnp.int32), axis=1)
    own_targets = lax.dynamic_slice_in_dim(destinations, first_unit, per_group)
    own_ranks = lax.dynamic_slice_in_dim(send_rank, first_unit, per_group)
    group_ids = jnp.arange(groups, dtype=jnp.int32)
    slot_ids = jnp.arange(CAP, dtype=jnp.int32)
    send_table = (
        (own_targets[None, None, :] == group_ids[:, None, None])
        & (own_ranks[None, None, :] == slot_ids[None, :, None])
    ).astype(jnp.bfloat16)
    arrive_ids = jnp.arange(per_group, dtype=jnp.int32)
    landing = (destinations == my_group)[None, :] & (arrival[None, :] == arrive_ids[:, None])
    recv_table = jnp.sum(
        (
            landing[:, None, None, :]
            & (source_group[None, None, None, :] == group_ids[None, :, None, None])
            & (send_rank[None, None, None, :] == slot_ids[None, None, :, None])
        ).astype(jnp.int32),
        axis=3,
    ).astype(jnp.bfloat16)
    moved_langs = jnp.sum(landing.astype(jnp.int32) * lang_labels[None, :], axis=1)
    lang_tokens = jnp.broadcast_to(moved_langs[:, None], (per_group, UNIT)).reshape(tok_group)

    moved = lax.all_to_all(
        pack_units(send_table, mixed_units), "dp", split_axis=0, concat_axis=0, tiled=True
    )
    stream_cols = unpack_units(recv_table, moved).reshape(tok_group, columns)
    stream_cols, cot_full = lax.optimization_barrier((stream_cols, cot_full))
    stream_full = lax.all_gather(stream_cols, "tensor", axis=1, tiled=True)

    grad_hidden = lax.dot_general(
        cot_full, down_weight, (((1,), (1,)), ((), ())), preferred_element_type=jnp.float32
    )
    cot_parts = deal(cot_full, share)
    stream_full, grad_hidden, *cot_parts = after(stream_full, grad_hidden, *cot_parts)
    cot_all = jnp.concatenate(cot_parts, axis=0)

    stream_f = stream_full.astype(jnp.float32)
    scaled_full = (stream_f * pick_gains(lang_tokens, norm_gains)).astype(jnp.bfloat16)
    inv_rms = lax.rsqrt(jnp.sum(stream_f * stream_f, axis=1) / width_d + 1e-05)

    my_start = lax.axis_index("tensor") * rows_here
    stream_rows = lax.dynamic_slice_in_dim(stream_full, my_start, rows_here, 0).astype(jnp.float32)
    lang_rows = lax.dynamic_slice_in_dim(lang_tokens, my_start, rows_here)
    gain_rows = pick_gains(lang_rows, norm_gains)
    scaled_rows = (stream_rows * gain_rows).astype(jnp.bfloat16)
    rms_rows = lax.dynamic_slice_in_dim(inv_rms, my_start, rows_here, 0)

    gate_acc = jnp.dot(scaled_full, gate_weight, preferred_element_type=jnp.float32)
    scaled_up, *dealt = after(scaled_full, *deal(scaled_rows, share))
    gathered = lax.all_gather(jnp.stack(dealt, axis=0), "tensor", axis=0)
    up_acc = jnp.dot(scaled_up, up_weight, preferred_element_type=jnp.float32)
    act_gate = inv_rms[:, None] * gate_acc
    act_up = inv_rms[:, None] * up_acc
    sigma = jax.nn.sigmoid(act_gate)
    silu = act_gate * sigma
    hidden = (silu * act_up).astype(jnp.bfloat16)
    weighted = inv_rms[:, None] * grad_hidden
    grad_gate = (weighted * act_up * sigma * (1.0 + act_gate * (1.0 - sigma))).astype(jnp.bfloat16)
    grad_up = (weighted * silu).astype(jnp.bfloat16)

    def over_tokens(left, right):
        return lax.dot_general(
            left, right, (((0,), (0,)), ((), ())), preferred_element_type=jnp.float32
        ).astype(jnp.bfloat16)

    def times_transposed(left, weight):
        return lax.dot_general(
            left, weight, (((1,), (1,)), ((), ())), preferred_element_type=jnp.float32
        )

    def scatter_rows(part):
        return lax.psum_scatter(
            part.astype(jnp.bfloat16), "tensor", scatter_dimension=0, tiled=True
        ).astype(jnp.float32)

    hidden_near = first_hops(hidden)
    out_part = jnp.dot(hidden, down_weight, preferred_element_type=jnp.float32)
    out_part, gathered = after(out_part, gathered)
    out_total = scatter_rows(out_part)
    scaled_all = gathered.transpose(1, 0, 2, 3).reshape(groups * tok_group, share)
    back_gate = times_transposed(grad_gate, gate_weight)

    grad_gate, grad_up, back_gate, *hidden_near = after(grad_gate, grad_up, back_gate, *hidden_near)
    gate_near = first_hops(grad_gate)
    hidden_far = second_hops(hidden_near)
    back_total = scatter_rows(back_gate + times_transposed(grad_up, up_weight))

    grad_up, *gate_near = after(grad_up, *gate_near)
    up_near = first_hops(grad_up)
    gate_far = second_hops(gate_near)
    down_grad = over_tokens(jnp.concatenate([hidden, *hidden_near, *hidden_far], axis=0), cot_all)

    up_near = after(*up_near)
    up_far = second_hops(up_near)
    gate_grad = over_tokens(scaled_all, jnp.concatenate([grad_gate, *gate_near, *gate_far], axis=0))
    up_grad = over_tokens(scaled_all, jnp.concatenate([grad_up, *up_near, *up_far], axis=0))

    layer_out = (stream_rows + out_total).astype(jnp.bfloat16)
    dot_sum = jnp.sum(scaled_rows.astype(jnp.float32) * back_total, axis=1)
    input_grad = (
        out_cotangent.astype(jnp.float32)
        + gain_rows * back_total
        - (rms_rows * rms_rows / width_d)[:, None] * stream_rows * dot_sum[:, None]
    ).astype(jnp.bfloat16)
    return (layer_out, input_grad, gate_grad, up_grad, down_grad)


def solution(mesh):
    return jax.shard_map(
        per_device,
        mesh=mesh,
        in_specs=(
            P("dp", "tensor"),
            P("dp", "tensor"),
            P("dp", "tensor"),
            P("dp", "tensor"),
            P(),
            P(),
            P(),
            P(),
            P(None, "tensor"),
            P(None, "tensor"),
            P("tensor", None),
            P(("dp", "tensor"), None),
        ),
        out_specs=(
            P(("dp", "tensor"), None),
            P(("dp", "tensor"), None),
            P("dp", "tensor"),
            P("dp", "tensor"),
            P("tensor", "dp"),
        ),
        check_vma=False,
    )
```

time: 459 us -> 297 us (0.65); the launches traced: 452 us -> 297 us
  waiting for transfers between devices: 206 us -> 118 us
  matrix products: 129 us -> 84.8 us
  other arithmetic: 38.8 us -> 20 us
  starting transfers between devices: 33.2 us -> 25.1 us
  local copies, waits for them, and re-layouts: 29.7 us -> 34.3 us
    all_to_all x7 -> x1, waiting for transfers between devices: 179 us -> 6.31 us  [per_device(): lax.all_to_all(pack_units(send_table, mixed_units), 'dp', split_axis=0, c...]
    ppermute x0 -> x18, waiting for transfers between devices: none -> 89.3 us  [exchange(): return lax.ppermute(block, 'dp', [(i, i ^ distance) for i in range(groups)])]
    dot_general x9 -> x8, matrix products: 111 us -> 72.4 us  [the longest x3 25 us: over_tokens(): lax.dot_general(left, right, (((0,), (0,)), ((), ())), preferred_element_...]
    all_to_all x7 -> x1, starting transfers between devices: 33.1 us -> 5.16 us  [per_device(): lax.all_to_all(pack_units(send_table, mixed_units), 'dp', split_axis=0, c...]
    reduce_sum x6 -> x4, other arithmetic: 27.2 us -> 7.03 us  [the longest x1 4.45 us: per_device(): inv_rms = lax.rsqrt(jnp.sum(stream_f * stream_f, axis=1) / width_d + 1e-05)]
    ppermute x0 -> x18, starting transfers between devices: none -> 19.1 us  [exchange(): return lax.ppermute(block, 'dp', [(i, i ^ distance) for i in range(groups)])]
    unnamed x24 -> x48, local copies, waits for them, and re-layouts: 0.64 us -> 14.8 us
    convert_element_type x3 -> x4, other arithmetic: 1.32 us -> 8.82 us  [the longest x1 4.83 us: per_device(): grad_up = (weighted * silu).astype(jnp.bfloat16)]
  transfers between devices with their start and end apart: 10 -> 24, of which waited for: 6 -> 10; matrix products, arithmetic and copies ran while one was open for 41% -> 41% of each run, Pallas kernels for 0% -> 0%
where the time goes in v1:
time: 297 us
  waiting for transfers between devices  118 us (40%)
  matrix products  84.8 us (29%)
  local copies, waits for them, and re-layouts  34.3 us (12%)
  starting transfers between devices  25.1 us (8%)
  other arithmetic  20 us (7%)
  between operations  14.3 us (5%)
    ppermute x18, waiting for transfers between devices, exchange(): return lax.ppermute(block, 'dp', [(i, i ^ distance) for i in range(groups)])  89.3 us
    dot_general x3, matrix products, over_tokens(): lax.dot_general(left, right, (((0,), (0,)), ((), ())), preferred_element_...  25 us
    all_gather x1, waiting for transfers between devices, per_device(): cot_full = lax.all_gather(out_cotangent, 'tensor', axis=0, tiled=True)  21.6 us
    ppermute x18, starting transfers between devices, exchange(): return lax.ppermute(block, 'dp', [(i, i ^ distance) for i in range(groups)])  19.1 us
    dot_general x2, matrix products, times_transposed(): lax.dot_general(left, weight, (((1,), (1,)), ((), ())), preferred_element...  18.8 us
    unnamed x48, local copies, waits for them, and re-layouts  14.8 us
    dot_general x1, matrix products, per_device(): lax.dot_general(cot_full, down_weight, (((1,), (1,)), ((), ())), preferre...  11.1 us
    dot_general x1, matrix products, per_device(): out_part = jnp.dot(hidden, down_weight, preferred_element_type=jnp.float32)  10.6 us
  transfers between devices with their start and end apart: 24, of which 10 were waited for; matrix products, arithmetic and copies ran while one was open for 41% of the time, Pallas kernels for 0%

profile of v1, /device:TPU:0, one launch (start us, length us, event | category | flops | bytes accessed | tf_op | source)
XLA Modules:
  0.0 296.6 jit_solution(606656558436712508)
XLA Ops:
  15.7 5.2 %all-to-all-start = ((bf16[4,2,48,512]{3,1,2,0:T(2,128)(2,1)}), bf16[4,2,48,512]{3,1,2,0:T(2,128)(2,1)S(1)}, u32[]{:S(2)}, u32[]{:S(2)}) async-start(bf16[4,2,48,512]{3,1,2,0:T(2,128)(2,1)} %copy.57), calls=%async_computation | async-start | bytes 786432 | tf_op jit(solution)/shard_map/all_to_all | solution.py:166
  21.2 6.3 %all-to-all-done = bf16[4,2,48,512]{3,1,2,0:T(2,128)(2,1)S(1)} async-done(((bf16[4,2,48,512]{3,1,2,0:T(2,128)(2,1)}), bf16[4,2,48,512]{3,1,2,0:T(2,128)(2,1)S(1)}, u32[]{:S(2)}, u32[]{:S(2)}) %all-to-all-start) | async-done | bytes 393248 | tf_op jit(solution)/shard_map/all_to_all | solution.py:166
  29.0 21.6 %all-gather.5.cloned.1.call-done = bf16[384,4096]{1,0:T(8,128)(2,1)} async-done(((bf16[48,4096]{1,0:T(8,128)(2,1)}), bf16[384,4096]{1,0:T(8,128)(2,1)}) %all-gather.5.cloned.1.call-update) | async-done | bytes 3145744 | tf_op jit(solution)/shard_map/all_gather | solution.py:126
  51.4 3.3 %constant_dynamic-slice_fusion.4 = (bf16[384,1024]{1,0:T(8,128)(2,1)S(1)}, bf16[384,1024]{1,0:T(8,128)(2,1)S(1)}, bf16[384,1024]{1,0:T(8,128)(2,1)S(1)}, bf16[384,1024]{1,0:T(8,128)(2,1)}) fusion(bf16[384,4096]{1,0:T(8,128)(2,1)} %all-gather.5.cloned.1.call-done, s32[]{:T(128)S(6)} %select_n.81, s32[]{:T(128)S(6)} %select_n.80, s32[]{:T(128)S(6)} %select_n.79, ...), kind=kLoop, calls=%fused_computation.91 | loop fusion | bytes 6291472 | tf_op jit(solution)/shard_map/dynamic_slice | solution.py:88
  58.2 11.1 %fusion.47 = f32[384,1792]{1,0:T(8,128)} fusion(bf16[384,4096]{1,0:T(8,128)(2,1)S(1)} %copy-done.2, bf16[1792,4096]{1,0:T(8,128)(2,1)} %param.22), kind=kOutput, calls=%fused_computation.122 | convolution fusion | flops 5637144576 | bytes 20578304 | tf_op jit(solution)/shard_map/dot_general | solution.py:173
  69.3 5.7 %collective-permute-done = bf16[384,1024]{1,0:T(8,128)(2,1)S(1)} collective-permute-done((bf16[384,1024]{1,0:T(8,128)(2,1)S(1)}, bf16[384,1024]{1,0:T(8,128)(2,1)S(1)}, u32[]{:S(2)}, u32[]{:S(2)}) %collective-permute-start) | collective-permute-done | bytes 786464 | tf_op jit(solution)/shard_map/ppermute | solution.py:63
  75.1 17.5 %collective-permute-done.1 = bf16[384,1024]{1,0:T(8,128)(2,1)} collective-permute-done((bf16[384,1024]{1,0:T(8,128)(2,1)S(1)}, bf16[384,1024]{1,0:T(8,128)(2,1)}, u32[]{:S(2)}, u32[]{:S(2)}) %collective-permute-start.1) | collective-permute-done | bytes 786464 | tf_op jit(solution)/shard_map/ppermute | solution.py:63
  92.5 4.5 %fusion.1 = (f32[384]{0:T(512)S(1)}, bf16[384,4096]{1,0:T(8,128)(2,1)S(1)}) fusion(bf16[384,4096]{1,0:T(8,128)(2,1)} %all-gather.7.cloned.1.call-done, f32[4096]{0:T(1024)S(1)} %bitcast.70, pred[384]{0:T(512)(128)(4,1)S(1)} %get-tuple-element.80, f32[4096]{0:T(1024)S(1)} %bitcast.74, pred[384]{0:T(512)(128)(4,1)S(1)} %get-tuple-element.81, ...), kind=kLoop, calls=%fused_computation.3 | loop fusion | flops 14155392 | bytes 6360064 | tf_op jit(solution)/shard_map/reduce_sum | solution.py:182
  102.1 9.6 %convolution_multiply_fusion.1 = f32[384,1792]{1,0:T(8,128)S(1)} fusion(bf16[384,4096]{1,0:T(8,128)(2,1)S(1)} %get-tuple-element.33, bf16[4096,1792]{1,0:T(8,128)(2,1)} %param.20, f32[384]{0:T(512)S(1)} %add_rsqrt_fusion), kind=kOutput, calls=%fused_computation.17 | convolution fusion | flops 5637832704 | bytes 20579840 | tf_op jit(solution)/shard_map/dot_general | solution.py:191
  111.7 7.9 %constant_dynamic-update-slice_fusion.14 = (bf16[1536,1792]{1,0:T(8,128)(2,1)}, bf16[384,1792]{1,0:T(8,128)(2,1)}, f32[384,1792]{1,0:T(8,128)}) fusion(f32[384,1792]{1,0:T(8,128)S(1)} %convolution_multiply_fusion.1, bf16[384,4096]{1,0:T(8,128)(2,1)S(1)} %get-tuple-element.33, bf16[4096,1792]{1,0:T(8,128)(2,1)S(1)} %bitcast.86, f32[384]{0:T(512)S(1)} %add_rsqrt_fusion), kind=kOutput, calls=%fused_computation.69 | convolution fusion | flops 5641961472 | bytes 26084864 | tf_op jit(solution)/shard_map/dot_general | solution.py:194
  122.8 4.8 %multiply_convert_fusion = (bf16[384,1792]{1,0:T(8,128)(2,1)S(1)}, bf16[384,1792]{1,0:T(8,128)(2,1)S(1)}) fusion(f32[384,1792]{1,0:T(8,128)} %fusion.47, f32[384]{0:T(512)S(1)} %add_rsqrt_fusion, f32[384,1792]{1,0:T(8,128)} %copy-done.4, f32[384,1792]{1,0:T(8,128)} %get-tuple-element.88), kind=kLoop, calls=%fused_computation.18 | loop fusion | flops 9633792 | bytes 11011584 | tf_op jit(solution)/shard_map/convert_element_type | solution.py:202
  127.6 9.5 %fusion.49 = f32[384,4096]{1,0:T(8,128)S(1)} fusion(bf16[384,1792]{1,0:T(8,128)(2,1)S(1)} %get-tuple-element.43, bf16[4096,1792]{1,0:T(8,128)(2,1)} %param.20), kind=kOutput, calls=%fused_computation.124 | convolution fusion | flops 5637144576 | bytes 22347776 | tf_op jit(solution)/shard_map/dot_general | solution.py:210
  137.1 13.2 %collective-permute-done.6 = bf16[384,1792]{1,0:T(8,128)(2,1)} collective-permute-done((bf16[384,1792]{1,0:T(8,128)(2,1)}, bf16[384,1792]{1,0:T(8,128)(2,1)}, u32[]{:S(2)}, u32[]{:S(2)}) %collective-permute-start.6) | collective-permute-done | bytes 1376288 | tf_op jit(solution)/shard_map/ppermute | solution.py:63
  151.5 9.3 %fusion.50 = f32[384,4096]{1,0:T(8,128)S(1)} fusion(bf16[384,1792]{1,0:T(8,128)(2,1)S(1)} %get-tuple-element.46, bf16[4096,1792]{1,0:T(8,128)(2,1)} %param.21), kind=kOutput, calls=%fused_computation.125 | convolution fusion | flops 5637144576 | bytes 22347776 | tf_op jit(solution)/shard_map/dot_general | solution.py:210
  168.3 10.6 %fusion.48 = bf16[384,4096]{1,0:T(8,128)(2,1)} fusion(bf16[384,1792]{1,0:T(8,128)(2,1)} %get-tuple-element.58, bf16[1792,4096]{1,0:T(8,128)(2,1)} %param.22), kind=kOutput, calls=%fused_computation.123 | convolution fusion | flops 5637144576 | bytes 19202048 | tf_op jit(solution)/shard_map/dot_general | solution.py:220
  181.6 2.6 constant_dynamic-update-slice_fusion.13
  184.2 3.4 %constant_dynamic-update-slice_fusion.4 = (bf16[1536,1792]{1,0:T(8,128)(2,1)}, bf16[1536,1792]{1,0:T(8,128)(2,1)}) fusion(bf16[384,1792]{1,0:T(8,128)(2,1)S(1)} %get-tuple-element.43, bf16[1536,1792]{1,0:T(8,128)(2,1)} %constant_dynamic-update-slice_fusion.13, bf16[384,1792]{1,0:T(8,128)(2,1)} %collective-permute-done.7), kind=kLoop, calls=%fused_computation.59 | loop fusion | bytes 5505024
  187.7 20.5 %collective-permute-done.16 = bf16[192,1792]{1,0:T(8,128)(2,1)S(1)} collective-permute-done((bf16[192,1792]{1,0:T(8,128)(2,1)}, bf16[192,1792]{1,0:T(8,128)(2,1)S(1)}, u32[]{:S(2)}, u32[]{:S(2)}) %collective-permute-start.16) | collective-permute-done | bytes 688160 | tf_op jit(solution)/shard_map/ppermute | solution.py:63
  211.8 9.6 %convolution_convert_fusion = bf16[1792,1024]{1,0:T(8,128)(2,1)} fusion(bf16[1536,1792]{1,0:T(8,128)(2,1)} %constant_dynamic-update-slice_fusion.10, bf16[384,1024]{1,0:T(8,128)(2,1)} %collective-permute-done.2, bf16[384,1024]{1,0:T(8,128)(2,1)} %collective-permute-done.1, bf16[384,1024]{1,0:T(8,128)(2,1)S(1)} %copy-done.12, bf16[384,1024]{1,0:T(8,128)(2,1)S(1)} %copy-done.6), kind=kOutput, calls=%fused_computation.6 | convolution fusion | flops 5651562496 | bytes 12320768 | tf_op jit(solution)/shard_map/dot_general | solution.py:205
  232.0 23.4 %collective-permute-done.10 = bf16[192,1792]{1,0:T(8,128)(2,1)S(1)} collective-permute-done((bf16[192,1792]{1,0:T(8,128)(2,1)}, bf16[192,1792]{1,0:T(8,128)(2,1)S(1)}, u32[]{:S(2)}, u32[]{:S(2)}) %collective-permute-start.10) | collective-permute-done | bytes 688160 | tf_op jit(solution)/shard_map/ppermute | solution.py:63
  262.0 7.0 %collective-permute-done.14 = bf16[192,1792]{1,0:T(8,128)(2,1)S(1)} collective-permute-done((bf16[192,1792]{1,0:T(8,128)(2,1)S(1)}, bf16[192,1792]{1,0:T(8,128)(2,1)S(1)}, u32[]{:S(2)}, u32[]{:S(2)}) %collective-permute-start.14) | collective-permute-done | bytes 688160 | tf_op jit(solution)/shard_map/ppermute | solution.py:63
  270.4 7.7 %convolution_convert_fusion.2 = bf16[1024,1792]{1,0:T(8,128)(2,1)} fusion(bf16[1536,1024]{1,0:T(8,128)(2,1)S(1)} %bitcast.59, bf16[1536,1792]{1,0:T(8,128)(2,1)S(1)} %bitcast.81), kind=kOutput, calls=%fused_computation.8 | convolution fusion | flops 5638979584 | bytes 12320768 | tf_op jit(solution)/shard_map/dot_general | solution.py:205
  278.1 7.7 %convolution_convert_fusion.1 = bf16[1024,1792]{1,0:T(8,128)(2,1)} fusion(bf16[1536,1024]{1,0:T(8,128)(2,1)S(1)} %bitcast.60, bf16[1536,1792]{1,0:T(8,128)(2,1)S(1)} %constant_dynamic-update-slice_fusion.5), kind=kOutput, calls=%fused_computation.7 | convolution fusion | flops 5638979584 | bytes 12320768 | tf_op jit(solution)/shard_map/dot_general | solution.py:205
  287.4 2.6 fusion.17
  (143 shorter events, 57.6 us)
Async XLA Ops:
  7.2 43.5 %all-gather.5.cloned.1.call-start = ((), (), s32[]{:S(2)}) async-start(), calls=%async_computation.3 | async-start | bytes 3538944 | tf_op jit(solution)/shard_map/all_gather | solution.py:126
  15.7 11.8 %all-to-all-start = ((bf16[4,2,48,512]{3,1,2,0:T(2,128)(2,1)}), bf16[4,2,48,512]{3,1,2,0:T(2,128)(2,1)S(1)}, u32[]{:S(2)}, u32[]{:S(2)}) async-start(bf16[4,2,48,512]{3,1,2,0:T(2,128)(2,1)} %copy.57), calls=%async_computation | async-start | bytes 786432 | tf_op jit(solution)/shard_map/all_to_all | solution.py:166
  20.9 71.7 %all-gather.7.cloned.1.call-start = ((), (), s32[]{:S(2)}) async-start(), calls=%async_computation.4 | async-start | bytes 3538944 | tf_op jit(solution)/shard_map/all_gather | solution.py:171
  50.7 174.4 %all-gather.9.cloned.1.call-start = ((), (), s32[]{:S(2)}) async-start(), calls=%async_computation.7 | async-start | bytes 3538944 | tf_op jit(solution)/shard_map/all_gather | solution.py:193
  54.7 20.4 %collective-permute-start = (bf16[384,1024]{1,0:T(8,128)(2,1)S(1)}, bf16[384,1024]{1,0:T(8,128)(2,1)S(1)}, u32[]{:S(2)}, u32[]{:S(2)}) collective-permute-start(bf16[384,1024]{1,0:T(8,128)(2,1)S(1)} %get-tuple-element.69), channel_id=1, source_target_pairs={{0,8},{8,0},{16,24},{24,16},{1,9},{9,1},{17,25},{25,17},{2,10},{10... | collective-permute-start | bytes 2359304 | tf_op jit(solution)/shard_map/ppermute | solution.py:63
  56.2 36.4 %collective-permute-start.1 = (bf16[384,1024]{1,0:T(8,128)(2,1)S(1)}, bf16[384,1024]{1,0:T(8,128)(2,1)}, u32[]{:S(2)}, u32[]{:S(2)}) collective-permute-start(bf16[384,1024]{1,0:T(8,128)(2,1)S(1)} %get-tuple-element.68), channel_id=1, source_target_pairs={{0,16},{8,24},{16,0},{24,8},{1,17},{9,25},{17,1},{25,9},{2,18},{10... | collective-permute-start | bytes 2359304 | tf_op jit(solution)/shard_map/ppermute | solution.py:63
  57.6 34.9 %collective-permute-start.2 = (bf16[384,1024]{1,0:T(8,128)(2,1)S(1)}, bf16[384,1024]{1,0:T(8,128)(2,1)}, u32[]{:S(2)}, u32[]{:S(2)}) collective-permute-start(bf16[384,1024]{1,0:T(8,128)(2,1)S(1)} %get-tuple-element.67), channel_id=1, source_target_pairs={{0,24},{8,16},{16,8},{24,0},{1,25},{9,17},{17,9},{25,1},{2,26},{10... | collective-permute-start | bytes 2359304 | tf_op jit(solution)/shard_map/ppermute | solution.py:63
  98.5 13.1 %collective-permute-start.3 = (bf16[48,1024]{1,0:T(8,128)(2,1)S(1)}, bf16[48,1024]{1,0:T(8,128)(2,1)S(1)}, u32[]{:S(2)}, u32[]{:S(2)}) collective-permute-start(bf16[48,1024]{1,0:T(8,128)(2,1)S(1)} %get-tuple-element.73), channel_id=1, source_target_pairs={{0,8},{8,0},{16,24},{24,16},{1,9},{9,1},{17,25},{25,17},{2,10},{10... | collective-permute-start | bytes 294920 | tf_op jit(solution)/shard_map/ppermute | solution.py:63
  99.7 11.9 %collective-permute-start.4 = (bf16[48,1024]{1,0:T(8,128)(2,1)S(1)}, bf16[48,1024]{1,0:T(8,128)(2,1)S(1)}, u32[]{:S(2)}, u32[]{:S(2)}) collective-permute-start(bf16[48,1024]{1,0:T(8,128)(2,1)S(1)} %get-tuple-element.72), channel_id=1, source_target_pairs={{0,16},{8,24},{16,0},{24,8},{1,17},{9,25},{17,1},{25,9},{2,18},{10... | collective-permute-start | bytes 294920 | tf_op jit(solution)/shard_map/ppermute | solution.py:63
  100.6 11.1 %collective-permute-start.5 = (bf16[48,1024]{1,0:T(8,128)(2,1)S(1)}, bf16[48,1024]{1,0:T(8,128)(2,1)S(1)}, u32[]{:S(2)}, u32[]{:S(2)}) collective-permute-start(bf16[48,1024]{1,0:T(8,128)(2,1)S(1)} %get-tuple-element.71), channel_id=1, source_target_pairs={{0,24},{8,16},{16,8},{24,0},{1,25},{9,17},{17,9},{25,1},{2,26},{10... | collective-permute-start | bytes 294920 | tf_op jit(solution)/shard_map/ppermute | solution.py:63
  119.6 30.7 %collective-permute-start.6 = (bf16[384,1792]{1,0:T(8,128)(2,1)}, bf16[384,1792]{1,0:T(8,128)(2,1)}, u32[]{:S(2)}, u32[]{:S(2)}) collective-permute-start(bf16[384,1792]{1,0:T(8,128)(2,1)} %get-tuple-element.58), channel_id=1, source_target_pairs={{0,8},{8,0},{16,24},{24,16},{1,9},{9,1},{17,25},{25,17},{2,10},{10... | collective-permute-start | bytes 4128776 | tf_op jit(solution)/shard_map/ppermute | solution.py:63
  120.8 30.7 %collective-permute-start.7 = (bf16[384,1792]{1,0:T(8,128)(2,1)}, bf16[384,1792]{1,0:T(8,128)(2,1)}, u32[]{:S(2)}, u32[]{:S(2)}) collective-permute-start(bf16[384,1792]{1,0:T(8,128)(2,1)} %get-tuple-element.58), channel_id=1, source_target_pairs={{0,16},{8,24},{16,0},{24,8},{1,17},{9,25},{17,1},{25,9},{2,18},{10... | collective-permute-start | bytes 4128776 | tf_op jit(solution)/shard_map/ppermute | solution.py:63
  122.5 163.3 %reduce-scatter.5.cloned.1.call-start = ((), (), s32[]{:S(2)}) async-start(), calls=%async_computation.6 | async-start | bytes 3538944 | tf_op jit(solution)/shard_map/reduce_scatter | solution.py:215
  163.3 124.1 %reduce-scatter.3.cloned.1.call-start = ((), (), s32[]{:S(2)}) async-start(), calls=%async_computation.5 | async-start | bytes 3538944 | tf_op jit(solution)/shard_map/reduce_scatter | solution.py:215
  163.7 46.3 %collective-permute-start.8 = (bf16[384,1792]{1,0:T(8,128)(2,1)S(1)}, bf16[384,1792]{1,0:T(8,128)(2,1)}, u32[]{:S(2)}, u32[]{:S(2)}) collective-permute-start(bf16[384,1792]{1,0:T(8,128)(2,1)S(1)} %get-tuple-element.43), channel_id=1, source_target_pairs={{0,8},{8,0},{16,24},{24,16},{1,9},{9,1},{17,25},{25,17},{2,10},{10... | collective-permute-start | bytes 4128776 | tf_op jit(solution)/shard_map/ppermute | solution.py:63
  164.3 45.7 %collective-permute-start.9 = (bf16[384,1792]{1,0:T(8,128)(2,1)S(1)}, bf16[384,1792]{1,0:T(8,128)(2,1)}, u32[]{:S(2)}, u32[]{:S(2)}) collective-permute-start(bf16[384,1792]{1,0:T(8,128)(2,1)S(1)} %get-tuple-element.43), channel_id=1, source_target_pairs={{0,16},{8,24},{16,0},{24,8},{1,17},{9,25},{17,1},{25,9},{2,18},{10... | collective-permute-start | bytes 4128776 | tf_op jit(solution)/shard_map/ppermute | solution.py:63
  167.7 40.5 %collective-permute-start.16 = (bf16[192,1792]{1,0:T(8,128)(2,1)}, bf16[192,1792]{1,0:T(8,128)(2,1)S(1)}, u32[]{:S(2)}, u32[]{:S(2)}) collective-permute-start(bf16[192,1792]{1,0:T(8,128)(2,1)} %slice.42), channel_id=1, source_target_pairs={{0,16},{8,24},{16,0},{24,8},{1,17},{9,25},{17,1},{25,9},{2,18},{10... | collective-permute-start | bytes 2064392 | tf_op jit(solution)/shard_map/ppermute | solution.py:63
  180.1 29.0 %collective-permute-start.17 = (bf16[192,1792]{1,0:T(8,128)(2,1)S(1)}, bf16[192,1792]{1,0:T(8,128)(2,1)S(1)}, u32[]{:S(2)}, u32[]{:S(2)}) collective-permute-start(bf16[192,1792]{1,0:T(8,128)(2,1)S(1)} %slice.43), channel_id=1, source_target_pairs={{0,8},{8,0},{16,24},{24,16},{1,9},{9,1},{17,25},{25,17},{2,10},{10... | collective-permute-start | bytes 2064392 | tf_op jit(solution)/shard_map/ppermute | solution.py:63
  210.0 46.3 %collective-permute-start.12 = (bf16[384,1792]{1,0:T(8,128)(2,1)S(1)}, bf16[384,1792]{1,0:T(8,128)(2,1)S(1)}, u32[]{:S(2)}, u32[]{:S(2)}) collective-permute-start(bf16[384,1792]{1,0:T(8,128)(2,1)S(1)} %get-tuple-element.46), channel_id=1, source_target_pairs={{0,8},{8,0},{16,24},{24,16},{1,9},{9,1},{17,25},{25,17},{2,10},{10... | collective-permute-start | bytes 4128776 | tf_op jit(solution)/shard_map/ppermute | solution.py:63
  211.5 44.9 %collective-permute-start.13 = (bf16[384,1792]{1,0:T(8,128)(2,1)S(1)}, bf16[384,1792]{1,0:T(8,128)(2,1)}, u32[]{:S(2)}, u32[]{:S(2)}) collective-permute-start(bf16[384,1792]{1,0:T(8,128)(2,1)S(1)} %get-tuple-element.46), channel_id=1, source_target_pairs={{0,16},{8,24},{16,0},{24,8},{1,17},{9,25},{17,1},{25,9},{2,18},{10... | collective-permute-start | bytes 4128776 | tf_op jit(solution)/shard_map/ppermute | solution.py:63
  223.4 32.0 %collective-permute-start.10 = (bf16[192,1792]{1,0:T(8,128)(2,1)}, bf16[192,1792]{1,0:T(8,128)(2,1)S(1)}, u32[]{:S(2)}, u32[]{:S(2)}) collective-permute-start(bf16[192,1792]{1,0:T(8,128)(2,1)} %slice.38), channel_id=1, source_target_pairs={{0,16},{8,24},{16,0},{24,8},{1,17},{9,25},{17,1},{25,9},{2,18},{10... | collective-permute-start | bytes 2064392 | tf_op jit(solution)/shard_map/ppermute | solution.py:63
  226.4 30.4 %collective-permute-start.11 = (bf16[192,1792]{1,0:T(8,128)(2,1)S(1)}, bf16[192,1792]{1,0:T(8,128)(2,1)S(1)}, u32[]{:S(2)}, u32[]{:S(2)}) collective-permute-start(bf16[192,1792]{1,0:T(8,128)(2,1)S(1)} %slice.39), channel_id=1, source_target_pairs={{0,8},{8,0},{16,24},{24,16},{1,9},{9,1},{17,25},{25,17},{2,10},{10... | collective-permute-start | bytes 2064392 | tf_op jit(solution)/shard_map/ppermute | solution.py:63
  256.4 12.6 %collective-permute-start.14 = (bf16[192,1792]{1,0:T(8,128)(2,1)S(1)}, bf16[192,1792]{1,0:T(8,128)(2,1)S(1)}, u32[]{:S(2)}, u32[]{:S(2)}) collective-permute-start(bf16[192,1792]{1,0:T(8,128)(2,1)S(1)} %slice.40), channel_id=1, source_target_pairs={{0,16},{8,24},{16,0},{24,8},{1,17},{9,25},{17,1},{25,9},{2,18},{10... | collective-permute-start | bytes 2064392 | tf_op jit(solution)/shard_map/ppermute | solution.py:63
  258.8 11.0 %collective-permute-start.15 = (bf16[192,1792]{1,0:T(8,128)(2,1)S(1)}, bf16[192,1792]{1,0:T(8,128)(2,1)S(1)}, u32[]{:S(2)}, u32[]{:S(2)}) collective-permute-start(bf16[192,1792]{1,0:T(8,128)(2,1)S(1)} %slice.41), channel_id=1, source_target_pairs={{0,8},{8,0},{16,24},{24,16},{1,9},{9,1},{17,25},{25,17},{2,10},{10... | collective-permute-start | bytes 2064392 | tf_op jit(solution)/shard_map/ppermute | solution.py:63
  (19 other events, 264.8 us)
Sparse Core Ops, SparseCore 0:
  9.7 40.9 all-gather.4
  52.9 37.1 all-gather.6
  122.6 36.3 all-gather.8
  163.4 38.2 reduce-scatter.4
  225.3 37.9 reduce-scatter.2
